TPU v7x, 32 devices: a whole 2x2x4 slice. The times are simulated.
32 devices in a mesh: row: 4 (over z), col: 8 (over y, x, core).
Axes of the slice: x: 2, y: 2, z: 4, core: 2. Of those that a mesh axis runs over, the one named last changes fastest.
Arguments:
- tokens: bfloat16 [8192, 1024], P(('row', 'col')), may hold values from -6 to 6
- out_grad: bfloat16 [8192, 1024], P(('row', 'col')), may hold values from -6 to 6
- expert_ids: int32 [8192], P(('row', 'col')), may hold values from 0 to 31, as said below
- router_logits: float32 [8192, 32], P(('row', 'col')), may hold values from -6 to 273
- router_weight: bfloat16 [32, 1024], P(('row', 'col')), may hold values from -0.1875 to 0.1875
- w_in: bfloat16 [32, 1024, 2048], P(('row', 'col')), may hold values from -0.1875 to 0.1875
- w_out: bfloat16 [32, 2048, 1024], P(('row', 'col')), may hold values from -0.125 to 0.125
Outputs:
- d_tokens: bfloat16 [8192, 1024], P(('row', 'col'))
- d_w_in: bfloat16 [32, 1024, 2048], P(('row', 'col'))
- d_w_out: bfloat16 [32, 2048, 1024], P(('row', 'col'))
- d_router: float32 [32, 1024], P(('row', 'col'))
Inputs may be any that keep to these rules, and one draw needn't show every extreme that they name: `expert_ids`: among the 256 tokens of one device no expert is chosen more than 16 times, and one expert is chosen exactly 16 times by the tokens of every device.
All inputs are finite; a program needn't handle non-finite values.
Results may differ from a plain program's by a relative error of at most 0.017.
Values may be sent and summed in bfloat16 or wider, within the bound.
A program may use at most 128 MiB of HBM per device.

v0:
```python
import jax
import jax.numpy as jnp
from jax import lax
from jax.sharding import PartitionSpec as P


def slot_layout(expert_ids, experts, capacity):
    onehot = (expert_ids[:, None] == jnp.arange(experts, dtype=jnp.int32)[None, :]).astype(
        jnp.int32
    )
    earlier = jnp.cumsum(onehot, axis=0) - onehot
    ranks = jnp.sum(earlier * onehot, axis=1)
    return (onehot, expert_ids * capacity + ranks)


def expert_pass(routed, scaled_rows, inner_weight, outer_weight):
    pre_act = jnp.dot(routed, inner_weight, preferred_element_type=jnp.float32)
    hidden = jnp.maximum(pre_act, 0.0).astype(jnp.bfloat16)
    expert_out = jnp.dot(hidden, outer_weight, preferred_element_type=jnp.float32).astype(
        jnp.bfloat16
    )
    back = jnp.dot(scaled_rows, outer_weight.T, preferred_element_type=jnp.float32)
    hidden_grad = jnp.where(pre_act > 0.0, back, 0.0).astype(jnp.bfloat16)
    grad_in = jnp.dot(hidden_grad, inner_weight.T, preferred_element_type=jnp.float32).astype(
        jnp.bfloat16
    )
    return (hidden, hidden_grad, expert_out, grad_in)


def weight_grads(routed, scaled_rows, hidden, hidden_grad):
    grad_inner = jnp.dot(routed.T, hidden_grad, preferred_element_type=jnp.float32).astype(
        jnp.bfloat16
    )
    grad_outer = jnp.dot(hidden.T, scaled_rows, preferred_element_type=jnp.float32).astype(
        jnp.bfloat16
    )
    return (grad_inner, grad_outer)


def per_device(tokens, out_grad, expert_ids, router_logits, router_weight, w_in, w_out):
    n_row = lax.axis_size("row")
    n_col = lax.axis_size("col")
    experts = n_row * n_col
    tok_count, width = tokens.shape
    capacity = max(2, 2 * tok_count // experts)
    slots = experts * capacity
    onehot, slot = slot_layout(expert_ids, experts, capacity)
    chosen = onehot.astype(jnp.float32)
    probs = jax.nn.softmax(router_logits, axis=-1)
    gate = jnp.sum(probs * chosen, axis=1)
    send_rows = jnp.zeros((slots, width), jnp.bfloat16).at[slot].set(tokens)
    scaled = (gate[:, None] * out_grad.astype(jnp.float32)).astype(jnp.bfloat16)
    send_second = jnp.zeros((slots, width), jnp.bfloat16).at[slot].set(scaled)
    routed, second_rows = (
        lax.all_to_all(
            lax.all_to_all(
                send_rows.reshape(n_row, n_col, capacity, width),
                "row",
                split_axis=0,
                concat_axis=0,
                tiled=True,
            ),
            "col",
            split_axis=1,
            concat_axis=1,
            tiled=True,
        ),
        lax.all_to_all(
            lax.all_to_all(
                send_second.reshape(n_row, n_col, capacity, width),
                "row",
                split_axis=0,
                concat_axis=0,
                tiled=True,
            ),
            "col",
            split_axis=1,
            concat_axis=1,
            tiled=True,
        ),
    )
    routed = routed.reshape(slots, width)
    second_rows = second_rows.reshape(slots, width)
    inner_weight = w_in[0]
    outer_weight = w_out[0]
    hidden, hidden_grad, expert_out, grad_in = expert_pass(
        routed, second_rows, inner_weight, outer_weight
    )
    grad_inner, grad_outer = weight_grads(routed, second_rows, hidden, hidden_grad)
    back_in, back_out = (
        lax.all_to_all(
            lax.all_to_all(
                grad_in.reshape(n_row, n_col, capacity, width),
                "row",
                split_axis=0,
                concat_axis=0,
                tiled=True,
            ),
            "col",
            split_axis=1,
            concat_axis=1,
            tiled=True,
        ),
        lax.all_to_all(
            lax.all_to_all(
                expert_out.reshape(n_row, n_col, capacity, width),
                "row",
                split_axis=0,
                concat_axis=0,
                tiled=True,
            ),
            "col",
            split_axis=1,
            concat_axis=1,
            tiled=True,
        ),
    )
    back_in = back_in.reshape(slots, width)[slot]
    back_out = back_out.reshape(slots, width)[slot]
    gate_grad = jnp.sum(out_grad.astype(jnp.float32) * back_out.astype(jnp.float32), axis=1)
    logit_grad = ((gate_grad * gate)[:, None] * (chosen - probs)).astype(jnp.bfloat16)
    columns = logit_grad
    router_part = jnp.dot(
        columns,
        lax.all_gather(router_weight, ("row", "col"), axis=0, tiled=True),
        preferred_element_type=jnp.float32,
    )
    d_tokens = (back_in.astype(jnp.float32) + router_part).astype(jnp.bfloat16)
    columns = logit_grad
    d_router = lax.psum_scatter(
        jnp.dot(columns.T, tokens, preferred_element_type=jnp.float32),
        ("row", "col"),
        scatter_dimension=0,
        tiled=True,
    )
    return (d_tokens, grad_inner[None], grad_outer[None], d_router)


def solution(mesh):
    placed = (
        P(("row", "col"), None),
        P(("row", "col"), None),
        P(("row", "col")),
        P(("row", "col"), None),
        P(("row", "col"), None),
        P(("row", "col"), None, None),
        P(("row", "col"), None, None),
    )
    return jax.shard_map(
        per_device,
        mesh=mesh,
        in_specs=placed,
        out_specs=(
            P(("row", "col"), None),
            P(("row", "col"), None, None),
            P(("row", "col"), None, None),
            P(("row", "col"), None),
        ),
        check_vma=False,
    )
```

profile of v0, /device:TPU:0, one launch (start us, length us, event | category | flops | bytes accessed | tf_op | source)
XLA Modules:
  0.0 367.3 jit_solution(11382328009316167254)
XLA Ops:
  10.1 3.1 scatter_custom_fusion
  13.3 6.3 %all-to-all-start = ((bf16[4,8,16,1024]{3,2,1,0:T(8,128)(2,1)}), bf16[4,8,16,1024]{3,2,1,0:T(8,128)(2,1)S(1)}, u32[]{:S(2)}, u32[]{:S(2)}) async-start(bf16[4,8,16,1024]{3,2,1,0:T(8,128)(2,1)} %bitcast.2), calls=%async_computation | async-start | bytes 2097152 | tf_op jit(solution)/shard_map/all_to_all | solution.py:56
  22.0 3.2 scatter_custom_fusion.1
  25.2 20.1 %all-to-all-done = bf16[4,8,16,1024]{3,2,1,0:T(8,128)(2,1)S(1)} async-done(((bf16[4,8,16,1024]{3,2,1,0:T(8,128)(2,1)}), bf16[4,8,16,1024]{3,2,1,0:T(8,128)(2,1)S(1)}, u32[]{:S(2)}, u32[]{:S(2)}) %all-to-all-start) | async-done | bytes 1048608 | tf_op jit(solution)/shard_map/all_to_all | solution.py:56
  45.3 3.5 all-to-all-start.2
  49.9 24.1 %all-to-all-done.2 = bf16[4,8,16,1024]{3,2,1,0:T(8,128)(2,1)S(1)} async-done(((bf16[4,8,16,1024]{3,2,1,0:T(8,128)(2,1)}), bf16[4,8,16,1024]{3,2,1,0:T(8,128)(2,1)S(1)}, u32[]{:S(2)}, u32[]{:S(2)}) %all-to-all-start.2) | async-done | bytes 1048608 | tf_op jit(solution)/shard_map/all_to_all | solution.py:69
  74.0 3.7 %all-to-all-start.1 = ((bf16[4,8,16,1024]{3,2,0,1:T(8,128)(2,1)}), bf16[4,8,16,1024]{3,2,0,1:T(8,128)(2,1)S(1)}, u32[]{:S(2)}, u32[]{:S(2)}) async-start(bf16[4,8,16,1024]{3,2,0,1:T(8,128)(2,1)} %copy.29), calls=%async_computation.1 | async-start | bytes 2097152 | tf_op jit(solution)/shard_map/all_to_all | solution.py:55
  78.8 14.3 %all-to-all-done.1 = bf16[4,8,16,1024]{3,2,0,1:T(8,128)(2,1)S(1)} async-done(((bf16[4,8,16,1024]{3,2,0,1:T(8,128)(2,1)}), bf16[4,8,16,1024]{3,2,0,1:T(8,128)(2,1)S(1)}, u32[]{:S(2)}, u32[]{:S(2)}) %all-to-all-start.1) | async-done | bytes 1048608 | tf_op jit(solution)/shard_map/all_to_all | solution.py:55
  93.2 3.6 all-to-all-start.3
  96.9 4.9 %fusion.6 = f32[512,2048]{1,0:T(8,128)S(1)} fusion(bf16[512,1024]{1,0:T(8,128)(2,1)S(1)} %bitcast.55, bf16[1,1024,2048]{2,1,0:T(8,128)(2,1)} %param.12), kind=kOutput, calls=%fused_computation.10 | convolution fusion | flops 2147483648 | bytes 9437184 | tf_op jit(solution)/shard_map/dot_general | solution.py:17
  103.8 3.3 fusion.13
  107.2 4.9 %all-to-all-done.3 = bf16[4,8,16,1024]{3,2,0,1:T(8,128)(2,1)S(1)} async-done(((bf16[4,8,16,1024]{3,2,0,1:T(8,128)(2,1)}), bf16[4,8,16,1024]{3,2,0,1:T(8,128)(2,1)S(1)}, u32[]{:S(2)}, u32[]{:S(2)}) %all-to-all-start.3) | async-done | bytes 1048608 | tf_op jit(solution)/shard_map/all_to_all | solution.py:68
  112.1 3.7 %all-to-all-start.6 = ((bf16[4,8,16,1024]{3,2,1,0:T(8,128)(2,1)}), bf16[4,8,16,1024]{3,2,1,0:T(8,128)(2,1)S(1)}, u32[]{:S(2)}, u32[]{:S(2)}) async-start(bf16[4,8,16,1024]{3,2,1,0:T(8,128)(2,1)} %bitcast.10), calls=%async_computation.6 | async-start | bytes 2097152 | tf_op jit(solution)/shard_map/all_to_all | solution.py:105
  115.9 6.2 %select_convert_fusion = bf16[512,2048]{1,0:T(8,128)(2,1)S(1)} fusion(f32[512,2048]{1,0:T(8,128)} %copy-done.9, bf16[512,1024]{1,0:T(8,128)(2,1)S(1)} %bitcast.57, bf16[1,2048,1024]{2,1,0:T(8,128)(2,1)} %param.13), kind=kOutput, calls=%fused_computation.15 | convolution fusion | flops 2150629376 | bytes 11534336 | tf_op jit(solution)/shard_map/dot_general | solution.py:22
  123.5 3.4 fusion.10
  126.8 11.9 %all-to-all-done.6 = bf16[4,8,16,1024]{3,2,1,0:T(8,128)(2,1)S(1)} async-done(((bf16[4,8,16,1024]{3,2,1,0:T(8,128)(2,1)}), bf16[4,8,16,1024]{3,2,1,0:T(8,128)(2,1)S(1)}, u32[]{:S(2)}, u32[]{:S(2)}) %all-to-all-start.6) | async-done | bytes 1048608 | tf_op jit(solution)/shard_map/all_to_all | solution.py:105
  138.7 3.5 all-to-all-start.4
  143.3 23.9 %all-to-all-done.4 = bf16[4,8,16,1024]{3,2,1,0:T(8,128)(2,1)S(1)} async-done(((bf16[4,8,16,1024]{3,2,1,0:T(8,128)(2,1)}), bf16[4,8,16,1024]{3,2,1,0:T(8,128)(2,1)S(1)}, u32[]{:S(2)}, u32[]{:S(2)}) %all-to-all-start.4) | async-done | bytes 1048608 | tf_op jit(solution)/shard_map/all_to_all | solution.py:92
  167.2 5.2 %all-to-all-start.7 = ((bf16[4,8,16,1024]{3,2,0,1:T(8,128)(2,1)}), bf16[4,8,16,1024]{3,2,0,1:T(8,128)(2,1)S(1)}, u32[]{:S(2)}, u32[]{:S(2)}) async-start(bf16[4,8,16,1024]{3,2,0,1:T(8,128)(2,1)} %copy.35), calls=%async_computation.7 | async-start | bytes 2097152 | tf_op jit(solution)/shard_map/all_to_all | solution.py:104
  172.5 45.8 %all-gather = bf16[32,1,1024]{2,1,0:T(2,128)(2,1)S(1)} all-gather(bf16[1,1,1024]{2,1,0:T(2,128)(2,1)S(1)} %bitcast.60), channel_id=1, replica_groups=mesh['row'=4,'col'=8] {'row','col'}, dimensions={0}, use_global_device_ids=true | all-gather | bytes 67584 | tf_op jit(solution)/shard_map/all_gather | solution.py:125
  219.4 3.6 all-to-all-start.5
  223.0 7.0 %convert_bitcast_fusion = bf16[1,2048,1024]{2,1,0:T(8,128)(2,1)} fusion(bf16[512,1024]{1,0:T(8,128)(2,1)} %bitcast.58, f32[512,2048]{1,0:T(8,128)} %copy-done.9), kind=kOutput, calls=%fused_computation.12 | convolution fusion | flops 2151677952 | bytes 9437184 | tf_op jit(solution)/shard_map/dot_general | solution.py:34
  230.0 4.4 %convert_bitcast_fusion.1 = bf16[1,1024,2048]{2,1,0:T(8,128)(2,1)} fusion(bf16[512,1024]{1,0:T(8,128)(2,1)S(1)} %bitcast.56, bf16[512,2048]{1,0:T(8,128)(2,1)S(1)} %copy-done.11), kind=kOutput, calls=%fused_computation.13 | convolution fusion | flops 2149580800 | bytes 7340032 | tf_op jit(solution)/shard_map/dot_general | solution.py:31
  240.7 118.4 %all-reduce.3.cloned.1.call-done = f32[32,1024]{1,0:T(8,128)} async-done(((f32[32,1024]{1,0:T(8,128)}), f32[32,1024]{1,0:T(8,128)}) %all-reduce.3.cloned.1.call-update) | async-done | bytes 131088
  (54 shorter events, 20.7 us)
Async XLA Ops:
  13.3 32.0 %all-to-all-start = ((bf16[4,8,16,1024]{3,2,1,0:T(8,128)(2,1)}), bf16[4,8,16,1024]{3,2,1,0:T(8,128)(2,1)S(1)}, u32[]{:S(2)}, u32[]{:S(2)}) async-start(bf16[4,8,16,1024]{3,2,1,0:T(8,128)(2,1)} %bitcast.2), calls=%async_computation | async-start | bytes 2097152 | tf_op jit(solution)/shard_map/all_to_all | solution.py:56
  45.3 28.7 %all-to-all-start.2 = ((bf16[4,8,16,1024]{3,2,1,0:T(8,128)(2,1)}), bf16[4,8,16,1024]{3,2,1,0:T(8,128)(2,1)S(1)}, u32[]{:S(2)}, u32[]{:S(2)}) async-start(bf16[4,8,16,1024]{3,2,1,0:T(8,128)(2,1)} %bitcast.5), calls=%async_computation.2 | async-start | bytes 2097152 | tf_op jit(solution)/shard_map/all_to_all | solution.py:69
  74.0 19.1 %all-to-all-start.1 = ((bf16[4,8,16,1024]{3,2,0,1:T(8,128)(2,1)}), bf16[4,8,16,1024]{3,2,0,1:T(8,128)(2,1)S(1)}, u32[]{:S(2)}, u32[]{:S(2)}) async-start(bf16[4,8,16,1024]{3,2,0,1:T(8,128)(2,1)} %copy.29), calls=%async_computation.1 | async-start | bytes 2097152 | tf_op jit(solution)/shard_map/all_to_all | solution.py:55
  93.2 18.9 %all-to-all-start.3 = ((bf16[4,8,16,1024]{3,2,0,1:T(8,128)(2,1)}), bf16[4,8,16,1024]{3,2,0,1:T(8,128)(2,1)S(1)}, u32[]{:S(2)}, u32[]{:S(2)}) async-start(bf16[4,8,16,1024]{3,2,0,1:T(8,128)(2,1)} %copy.31), calls=%async_computation.3 | async-start | bytes 2097152 | tf_op jit(solution)/shard_map/all_to_all | solution.py:68
  96.8 5.0 %copy-start.1 = (bf16[4,8,16,1024]{3,2,1,0:T(8,128)(2,1)}, bf16[4,8,16,1024]{3,2,1,0:T(8,128)(2,1)S(1)}, u32[]{:S(2)}) copy-start(bf16[4,8,16,1024]{3,2,1,0:T(8,128)(2,1)S(1)} %copy.30) | copy-start | bytes 3145732
  96.8 7.0 %copy-start.7 = (bf16[1,2048,1024]{2,1,0:T(8,128)(2,1)S(1)}, bf16[1,2048,1024]{2,1,0:T(8,128)(2,1)}, u32[]{:S(2)}) copy-start(bf16[1,2048,1024]{2,1,0:T(8,128)(2,1)} %param.13) | copy-start | bytes 12582916
  101.8 2.0 copy-start.9
  112.1 26.6 %all-to-all-start.6 = ((bf16[4,8,16,1024]{3,2,1,0:T(8,128)(2,1)}), bf16[4,8,16,1024]{3,2,1,0:T(8,128)(2,1)S(1)}, u32[]{:S(2)}, u32[]{:S(2)}) async-start(bf16[4,8,16,1024]{3,2,1,0:T(8,128)(2,1)} %bitcast.10), calls=%async_computation.6 | async-start | bytes 2097152 | tf_op jit(solution)/shard_map/all_to_all | solution.py:105
  115.9 6.3 %copy-start.3 = (bf16[4,8,16,1024]{3,2,1,0:T(8,128)(2,1)}, bf16[4,8,16,1024]{3,2,1,0:T(8,128)(2,1)S(1)}, u32[]{:S(2)}) copy-start(bf16[4,8,16,1024]{3,2,1,0:T(8,128)(2,1)S(1)} %copy.32) | copy-start | bytes 3145732
  115.9 7.6 %copy-start.8 = (bf16[1,1024,2048]{2,1,0:T(8,128)(2,1)S(1)}, bf16[1,1024,2048]{2,1,0:T(8,128)(2,1)}, u32[]{:S(2)}) copy-start(bf16[1,1024,2048]{2,1,0:T(8,128)(2,1)} %param.12) | copy-start | bytes 12582916
  122.1 1.3 copy-start.10
  126.8 45.6 %copy-start.6 = (bf16[1,1024]{1,0:T(2,128)(2,1)S(1)}, bf16[1,1024]{1,0:T(2,128)(2,1)}, u32[]{:S(2)}) copy-start(bf16[1,1024]{1,0:T(2,128)(2,1)} %param.11) | copy-start | bytes 6148
  138.7 28.5 %all-to-all-start.4 = ((bf16[4,8,16,1024]{3,2,1,0:T(8,128)(2,1)}), bf16[4,8,16,1024]{3,2,1,0:T(8,128)(2,1)S(1)}, u32[]{:S(2)}, u32[]{:S(2)}) async-start(bf16[4,8,16,1024]{3,2,1,0:T(8,128)(2,1)} %bitcast.8), calls=%async_computation.4 | async-start | bytes 2097152 | tf_op jit(solution)/shard_map/all_to_all | solution.py:92
  167.2 52.1 %all-to-all-start.7 = ((bf16[4,8,16,1024]{3,2,0,1:T(8,128)(2,1)}), bf16[4,8,16,1024]{3,2,0,1:T(8,128)(2,1)S(1)}, u32[]{:S(2)}, u32[]{:S(2)}) async-start(bf16[4,8,16,1024]{3,2,0,1:T(8,128)(2,1)} %copy.35), calls=%async_computation.7 | async-start | bytes 2097152 | tf_op jit(solution)/shard_map/all_to_all | solution.py:104
  219.4 18.9 %all-to-all-start.5 = ((bf16[4,8,16,1024]{3,2,0,1:T(8,128)(2,1)}), bf16[4,8,16,1024]{3,2,0,1:T(8,128)(2,1)S(1)}, u32[]{:S(2)}, u32[]{:S(2)}) async-start(bf16[4,8,16,1024]{3,2,0,1:T(8,128)(2,1)} %copy.33), calls=%async_computation.5 | async-start | bytes 2097152 | tf_op jit(solution)/shard_map/all_to_all | solution.py:91
  222.9 7.1 %copy-start.2 = (bf16[4,8,16,1024]{3,2,1,0:T(8,128)(2,1)S(1)}, bf16[4,8,16,1024]{3,2,1,0:T(8,128)(2,1)}, u32[]{:S(2)}) copy-start(bf16[4,8,16,1024]{3,2,1,0:T(8,128)(2,1)} %copy-done.1) | copy-start | bytes 3145732
  222.9 136.1 %all-reduce.3.cloned.1.call-start = ((), (), s32[]{:S(2)}) async-start(), calls=%async_computation.8 | async-start | bytes 262144
  223.0 7.1 %copy-start.11 = (bf16[512,2048]{1,0:T(8,128)(2,1)S(1)}, bf16[512,2048]{1,0:T(8,128)(2,1)}, u32[]{:S(2)}) copy-start(bf16[512,2048]{1,0:T(8,128)(2,1)} %copy-done.10) | copy-start | bytes 6291460
  234.5 1.5 copy-start.4
  234.5 1.5 copy-start.5
  234.6 1.2 copy-start
Sparse Core Ops, SparseCore 0:
  238.0 120.9 all-reduce.2
where the time goes:
time: 368 us; the launch traced here: 367 us
  waiting for transfers between devices  218 us (59%)
  blocking collectives  45.8 us (12%)
  starting transfers between devices  33.2 us (9%)
  matrix products  32.4 us (9%)
  local copies, waits for them, and re-layouts  15 us (4%)
  between operations  14.3 us (4%)
  other arithmetic  8.57 us (2%)
    unnamed x2, waiting for transfers between devices  118 us
    all_gather x1, blocking collectives, per_device(): lax.all_gather(router_weight, ('row', 'col'), axis=0, tiled=True)  45.8 us
    all_to_all x1, waiting for transfers between devices, per_device(): lax.all_to_all(send_second.reshape(n_row, n_col, capacity, width), 'row',...  24.1 us
    all_to_all x1, waiting for transfers between devices, per_device(): lax.all_to_all(grad_in.reshape(n_row, n_col, capacity, width), 'row', spl...  23.9 us
    all_to_all x1, waiting for transfers between devices, per_device(): lax.all_to_all(send_rows.reshape(n_row, n_col, capacity, width), 'row', s...  20.1 us
    all_to_all x1, waiting for transfers between devices, per_device(): lax.all_to_all(lax.all_to_all(send_rows.reshape(n_row, n_col, capacity, w...  14.3 us
    all_to_all x1, waiting for transfers between devices, per_device(): lax.all_to_all(expert_out.reshape(n_row, n_col, capacity, width), 'row',...  11.9 us
  transfers between devices with their start and end apart: 9, of which 8 were waited for; matrix products, arithmetic and copies ran while one was open for 12% of the time, Pallas kernels for 0%

commit v1 on v0

v1 whole, which is shorter than its diff:
```python
import functools

import jax
import jax.numpy as jnp
from jax import lax
from jax.experimental import pallas as pl
from jax.experimental.pallas import tpu as pltpu
from jax.sharding import PartitionSpec as P

MESH = pl.DeviceIdType.MESH
BF = jnp.bfloat16
F32 = jnp.float32


def dot(a, b, dims=((1,), (0,)), **kw):
    return lax.dot_general(a, b, (dims, ((), ())), preferred_element_type=F32, **kw)


def xor_row(row, dz):
    out, bit = 0, 1
    while bit < 8:
        out = out + bit * (((row // bit) % 2 + (dz // bit) % 2) % 2)
        bit *= 2
    return out


def kernel(
    n_row, n_col, cap, fb,
    tok_ref, og_ref, ids_ref, logit_ref, rw_ref, wi_hbm, wo_hbm,
    dtok_ref, drouter_ref, dwi_hbm, dwo_hbm,
    wi, wo, send_t, send_s, recv_t, recv_s, gout, gback, hid, hgr, acc,
    rwrecv, rwmat, scsend, screcv, scmat, drsend, drrecv,
    wsem, osem, ssem, rt_sem, rs_sem, rg_sem, small_sem,
):
    n = n_row * n_col
    row = lax.axis_index("row")
    col = lax.axis_index("col")
    me = row * n_col + col
    tok, width = tok_ref.shape
    ffn = wi.shape[1]
    crows = n_col * cap
    order = list(range(n_row - 1, -1, -1))

    def rows_of(dev):
        return pl.ds(pl.multiple_of(dev * cap, cap), cap)

    def chunk_of(r):
        return pl.ds(pl.multiple_of(r * crows, crows), crows)

    load_i = pltpu.make_async_copy(wi_hbm.at[0], wi, wsem.at[0])
    load_o = pltpu.make_async_copy(wo_hbm.at[0], wo, wsem.at[1])
    load_i.start()
    load_o.start()

    barrier = pltpu.get_barrier_semaphore()

    def others(body):
        def step(k, c):
            peer = lax.rem(me + k, n)
            body(peer, (peer // n_col, lax.rem(peer, n_col)))
            return c
        lax.fori_loop(1, n, step, 0)

    others(lambda peer, dev: pl.semaphore_signal(
        barrier, inc=1, device_id=dev, device_id_type=MESH))

    ids = ids_ref[...]
    lanes = lax.broadcasted_iota(jnp.int32, (tok, n), 1)
    chosen = (ids == lanes).astype(F32)
    logits = logit_ref[...]
    ex = jnp.exp(logits - jnp.max(logits, axis=1, keepdims=True))
    probs = ex / jnp.sum(ex, axis=1, keepdims=True)
    gate = jnp.sum(probs * chosen, axis=1, keepdims=True)
    it0 = lax.broadcasted_iota(jnp.int32, (tok, tok), 0)
    it1 = lax.broadcasted_iota(jnp.int32, (tok, tok), 1)
    earlier = dot((it1 < it0).astype(F32).astype(BF), chosen.astype(BF))
    rank = jnp.sum(earlier * chosen, axis=1, keepdims=True)
    slot = ids.astype(F32) * cap + rank
    slot_row = jnp.sum(jnp.where(it0 == it1, slot, 0.0), axis=0, keepdims=True)
    tokens = tok_ref[...]
    scaled = (gate * og_ref[...].astype(F32)).astype(BF)

    def fill(r):
        at = lax.broadcasted_iota(jnp.int32, (crows, tok), 0).astype(F32) + (
            r * crows).astype(F32)
        pick = (at == slot_row).astype(F32).astype(BF)
        send_t[chunk_of(r), :] = dot(pick, tokens).astype(BF)
        send_s[chunk_of(r), :] = dot(pick, scaled).astype(BF)

    def push(src, dst, sem, rsem, dev):
        pltpu.make_async_remote_copy(
            src_ref=src, dst_ref=dst, send_sem=sem, recv_sem=rsem,
            device_id=dev, device_id_type=MESH,
        ).start()

    def dispatch(dz, j):
        r = xor_row(row, dz)
        c = lax.rem(col + j, n_col)
        peer = r * n_col + c
        push(send_t.at[rows_of(peer)], recv_t.at[rows_of(me)], ssem.at[0], rt_sem.at[dz], (r, c))
        push(send_s.at[rows_of(peer)], recv_s.at[rows_of(me)], ssem.at[1], rs_sem.at[dz], (r, c))

    def col_loop(first, body):
        def step(j, c):
            body(j)
            return c
        lax.fori_loop(first, n_col, step, 0)

    half = n_row // 2
    phases = [(half, 0)] + [(half + i, i) for i in range(1, half)]
    first = True
    for far, near in phases:
        fill(xor_row(row, far))
        fill(xor_row(row, near))
        if first:
            pl.semaphore_wait(barrier, n - 1)
            first = False
        dispatch(far, 0)
        if near == 0:
            pltpu.make_async_copy(
                send_t.at[rows_of(me)], recv_t.at[rows_of(me)], rt_sem.at[0]).start()
            pltpu.make_async_copy(
                send_s.at[rows_of(me)], recv_s.at[rows_of(me)], rs_sem.at[0]).start()
        else:
            dispatch(near, 0)

        def both(j, far=far, near=near):
            dispatch(far, j)
            dispatch(near, j)
        col_loop(1, both)

    rwrecv[pl.ds(me, 1)] = rw_ref[...].astype(F32)[None]
    others(lambda peer, dev: push(
        rwrecv.at[me], rwrecv.at[me], ssem.at[3], small_sem.at[0], dev))

    load_i.wait()
    load_o.wait()

    def wait_rows(ref, sl, sem):
        pltpu.make_async_copy(ref.at[sl], ref.at[sl], sem).wait()

    eye = (lax.broadcasted_iota(jnp.int32, (crows, crows), 0)
           == lax.broadcasted_iota(jnp.int32, (crows, crows), 1))

    for near, far in [(b, a) for a, b in phases]:
        for dz in (near, far):
            r = xor_row(row, dz)
            sl = chunk_of(r)
            wait_rows(recv_t, sl, rt_sem.at[dz])
            wait_rows(recv_s, sl, rs_sem.at[dz])
            acc[...] = jnp.zeros_like(acc)

            def block(f, v, sl=sl):
                fs = pl.ds(pl.multiple_of(f * fb, fb), fb)
                w1 = wi[:, fs]
                pre = dot(recv_t[sl, :], w1)
                back = dot(recv_s[sl, :], wo[fs, :], ((1,), (1,)))
                h = jnp.maximum(pre, 0.0).astype(BF)
                g = jnp.where(pre > 0.0, back, 0.0).astype(BF)
                hid[sl, fs] = h
                hgr[sl, fs] = g
                acc[...] += dot(g, w1, ((1,), (1,)))
                return v + jnp.sum(h.astype(F32) * back, axis=1, keepdims=True)

            v = lax.fori_loop(0, ffn // fb, block, jnp.zeros((crows, 1), F32))
            gout[sl, :] = acc[...].astype(BF)
            scsend[pl.ds(r, 1)] = jnp.sum(
                jnp.where(eye, v, 0.0), axis=0, keepdims=True)[None]

            def give(j, r=r, dz=dz):
                c = lax.rem(col + j, n_col)
                peer = r * n_col + c
                push(scsend.at[r], screcv.at[me], ssem.at[4], small_sem.at[1], (r, c))
                push(gout.at[rows_of(peer)], gback.at[rows_of(me)], ssem.at[2], rg_sem.at[dz], (r, c))
            if dz == 0:
                pltpu.make_async_copy(
                    gout.at[rows_of(me)], gback.at[rows_of(me)], rg_sem.at[0]).start()
                pltpu.make_async_copy(
                    scsend.at[r], screcv.at[me], small_sem.at[1]).start()
                col_loop(1, give)
            else:
                col_loop(0, give)

    db = min(256, width)

    def grad_in_w(i, c):
        ds = pl.ds(pl.multiple_of(i * db, db), db)
        wi[ds, :] = dot(recv_t[:, ds], hgr[...], ((0,), (0,))).astype(BF)
        pltpu.make_async_copy(wi.at[ds], dwi_hbm.at[0, ds], osem.at[0]).start()
        return c
    lax.fori_loop(0, width // db, grad_in_w, 0)

    def grad_out_w(i, c):
        fs = pl.ds(pl.multiple_of(i * fb, fb), fb)
        wo[fs, :] = dot(hid[:, fs], recv_s[...], ((0,), (0,))).astype(BF)
        pltpu.make_async_copy(wo.at[fs], dwo_hbm.at[0, fs], osem.at[1]).start()
        return c
    lax.fori_loop(0, ffn // fb, grad_out_w, 0)

    pltpu.make_async_copy(screcv, screcv, small_sem.at[1]).wait()
    for e in range(n):
        scmat[e:e + 1, :] = screcv[e]
    picked = dot(chosen, scmat[...], precision=lax.Precision.HIGHEST)
    lane = lax.broadcasted_iota(jnp.int32, (tok, crows), 1).astype(F32)
    mine = (col * cap).astype(F32) + rank
    vg = jnp.sum(jnp.where(lane == mine, picked, 0.0), axis=1, keepdims=True)
    lg = (vg * (chosen - probs)).astype(BF)
    part = dot(lg, tokens, ((0,), (0,)))
    for e in range(n):
        drsend[e] = part[e:e + 1, :]
    others(lambda peer, dev: push(
        drsend.at[peer], drrecv.at[me], ssem.at[5], small_sem.at[2], dev))
    drrecv[pl.ds(me, 1)] = drsend[pl.ds(me, 1)]

    wait_rows(rwrecv, pl.ds(0, n - 1), small_sem.at[0])
    for e in range(n):
        rwmat[e:e + 1, :] = rwrecv[e]
    router_part = dot(lg, rwmat[...].astype(BF))
    for dz in order[::-1]:
        wait_rows(gback, chunk_of(xor_row(row, dz)), rg_sem.at[dz])
    at = lax.broadcasted_iota(jnp.int32, (tok, n * cap), 1).astype(F32)
    pick = (at == slot).astype(F32).astype(BF)
    dtok_ref[...] = (dot(pick, gback[...]) + router_part).astype(BF)

    wait_rows(drrecv, pl.ds(0, n - 1), small_sem.at[2])
    drouter_ref[...] = jnp.sum(drrecv[...], axis=0)

    most = pl.ds(0, (n - 1) * cap)
    wait_rows(send_t, most, ssem.at[0])
    wait_rows(send_s, most, ssem.at[1])
    wait_rows(gout, most, ssem.at[2])
    wait_rows(rwrecv, pl.ds(0, n - 1), ssem.at[3])
    wait_rows(screcv, pl.ds(0, n - 1), ssem.at[4])
    wait_rows(drsend, pl.ds(0, n - 1), ssem.at[5])
    pltpu.make_async_copy(wi, dwi_hbm.at[0], osem.at[0]).wait()
    pltpu.make_async_copy(wo, dwo_hbm.at[0], osem.at[1]).wait()


def per_device(tokens, out_grad, expert_ids, router_logits, router_weight, w_in, w_out):
    n_row = lax.axis_size("row")
    n_col = lax.axis_size("col")
    n = n_row * n_col
    tok, width = tokens.shape
    ffn = w_in.shape[2]
    cap = max(16, 2 * tok // n)
    rows = n * cap
    crows = n_col * cap
    vm = pl.BlockSpec(memory_space=pltpu.VMEM)
    hbm = pl.BlockSpec(memory_space=pl.ANY)
    dma = pltpu.SemaphoreType.DMA
    big = pltpu.VMEM((rows, width), BF)
    d_tokens, d_router, d_wi, d_wo = pl.pallas_call(
        functools.partial(kernel, n_row, n_col, cap, min(512, ffn)),
        out_shape=(
            jax.ShapeDtypeStruct((tok, width), BF),
            jax.ShapeDtypeStruct((1, width), F32),
            jax.ShapeDtypeStruct(w_in.shape, BF),
            jax.ShapeDtypeStruct(w_out.shape, BF),
        ),
        in_specs=[vm] * 5 + [hbm] * 2,
        out_specs=(vm, vm, hbm, hbm),
        scratch_shapes=[
            pltpu.VMEM((width, ffn), BF),
            pltpu.VMEM((ffn, width), BF),
            big, big, big, big, big, big,
            pltpu.VMEM((rows, ffn), BF),
            pltpu.VMEM((rows, ffn), BF),
            pltpu.VMEM((crows, width), F32),
            pltpu.VMEM((n, 1, width), F32),
            pltpu.VMEM((n, width), F32),
            pltpu.VMEM((n_row, 1, crows), F32),
            pltpu.VMEM((n, 1, crows), F32),
            pltpu.VMEM((n, crows), F32),
            pltpu.VMEM((n, 1, width), F32),
            pltpu.VMEM((n, 1, width), F32),
            dma((2,)),
            dma((2,)),
            dma((6,)),
            dma((n_row,)),
            dma((n_row,)),
            dma((n_row,)),
            dma((3,)),
        ],
        compiler_params=pltpu.CompilerParams(
            collective_id=0, has_side_effects=True, vmem_limit_bytes=60 * 1024 * 1024
        ),
        cost_estimate=pl.CostEstimate(
            flops=10 * rows * width * ffn, bytes_accessed=8 * width * ffn, transcendentals=0
        ),
    )(tokens, out_grad, expert_ids[:, None], router_logits, router_weight, w_in, w_out)
    return d_tokens, d_wi, d_wo, d_router


def solution(mesh):
    both = ("row", "col")
    flat, cube = P(both, None), P(both, None, None)
    return jax.shard_map(
        per_device,
        mesh=mesh,
        in_specs=(flat, flat, P(both), flat, flat, cube, cube),
        out_specs=(flat, cube, cube, flat),
        check_vma=False,
    )
```

time: 368 us -> 102 us (0.28)
  waiting for transfers between devices: 218 us -> 0 us
  Pallas kernels: 0 us -> 88.5 us
  blocking collectives: 45.8 us -> 0 us
  starting transfers between devices: 33.2 us -> 0 us
  matrix products: 32.4 us -> 0 us
  between operations: 14.3 us -> 0.64 us
  other arithmetic: 8.57 us -> 0 us
    unnamed x2 -> x0, waiting for transfers between devices: 118 us -> none
    all_to_all x8 -> x0, waiting for transfers between devices: 99.6 us -> none  [the longest x1 24.1 us: per_device(): lax.all_to_all(send_second.reshape(n_row, n_col, capacity, width), 'row',...]
    pallas_call x0 -> x1, Pallas kernels: none -> 88.5 us  [per_device(): pl.pallas_call(functools.partial(kernel, n_row, n_col, cap, min(512, ffn)...]
    all_gather x1 -> x0, blocking collectives: 45.8 us -> none  [per_device(): lax.all_gather(router_weight, ('row', 'col'), axis=0, tiled=True)]
    all_to_all x8 -> x0, starting transfers between devices: 33.1 us -> none  [the longest x1 6.32 us: per_device(): lax.all_to_all(send_rows.reshape(n_row, n_col, capacity, width), 'row', s...]
    dot_general x8 -> x0, matrix products: 32.4 us -> none  [the longest x1 7.04 us: weight_grads(): jnp.dot(hidden.T, scaled_rows, preferred_element_type=jnp.float32)]
    unnamed x25 -> x9, local copies, waits for them, and re-layouts: 4.75 us -> 10.9 us
    all_to_all x8 -> x0, local copies, waits for them, and re-layouts: 4.63 us -> none  [the longest x1 1.09 us: per_device(): lax.all_to_all(expert_out.reshape(n_row, n_col, capacity, width), 'row',...]
  transfers between devices with their start and end apart: 9 -> 0, of which waited for: 8 -> 0; matrix products, arithmetic and copies ran while one was open for 12% -> 0% of each run, Pallas kernels for 0% -> 0%
where the time goes in v1:
time: 102 us
  Pallas kernels  88.5 us (87%)
  local copies, waits for them, and re-layouts  12.4 us (12%)
    pallas_call x1, Pallas kernels, per_device(): pl.pallas_call(functools.partial(kernel, n_row, n_col, cap, min(512, ffn)...  88.5 us
    unnamed x9, local copies, waits for them, and re-layouts  10.9 us

profile of v1, /device:TPU:0, one launch (start us, length us, event | category | flops | bytes accessed | tf_op | source)
XLA Modules:
  0.0 101.6 jit_solution(8281622183462599905)
XLA Ops:
  0.6 1.5 %copy.12.ids_ref = s32[256,1]{1,0:T(8,128)} copy(s32[256,1]{0,1:T(1,128)} %bitcast.1) | data formatting | bytes 2048 | tf_op jit(solution)/shard_map/broadcast_in_dim | solution.py:290
  2.1 1.5 %copy.13.logit_ref = f32[256,32]{1,0:T(8,128)} copy(f32[256,32]{0,1:T(8,128)} %param.10) | data formatting | bytes 65536 | tf_op args[3]
  3.6 88.5 %shard_map.102 = (bf16[256,1024]{1,0:T(8,128)(2,1)}, f32[1,1024]{1,0:T(1,128)}, bf16[1,1024,2048]{2,1,0:T(8,128)(2,1)}, bf16[1,2048,1024]{2,1,0:T(8,128)(2,1)}) custom-call(bf16[256,1024]{1,0:T(8,128)(2,1)} %tok_ref.1, bf16[256,1024]{1,0:T(8,128)(2,1)} %og_ref.1, s32[256,1]{1,0:T(8,128)} %copy.12.ids_ref, f32[256,32]{1,0:T(8,128)} %copy.13.logit_ref, ...), custom_call_target="tpu_custom_call" | custom-call | flops 10737418240 | bytes 16777216 | tf_op jit(solution)/shard_map/pallas_call | solution.py:252
  92.2 1.9 %copy.18 = bf16[256,1024]{1,0:T(8,128)(2,1)} copy(bf16[256,1024]{1,0:T(8,128)(2,1)} %get-tuple-element.16) | data formatting | bytes 1048576
  94.0 0.0 copy-start
  94.0 4.9 %copy.19 = bf16[1,1024,2048]{2,1,0:T(8,128)(2,1)} copy(bf16[1,1024,2048]{2,1,0:T(8,128)(2,1)} %get-tuple-element.17) | data formatting | bytes 8388608
  99.0 0.0 copy-done
  99.0 0.0 copy-start.1
  99.0 2.0 %copy.20 = bf16[1,2048,1024]{2,1,0:T(8,128)(2,1)} copy(bf16[1,2048,1024]{2,1,0:T(8,128)(2,1)S(1)} %copy-done) | data formatting | bytes 8388608
  101.0 0.0 copy-done.1
  101.0 0.6 copy.21
Async XLA Ops:
  94.0 4.9 %copy-start = (bf16[1,2048,1024]{2,1,0:T(8,128)(2,1)S(1)}, bf16[1,2048,1024]{2,1,0:T(8,128)(2,1)}, u32[]{:S(2)}) copy-start(bf16[1,2048,1024]{2,1,0:T(8,128)(2,1)} %get-tuple-element.18) | copy-start | bytes 12582916
  99.0 2.0 %copy-start.1 = (f32[1,1024]{1,0:T(1,128)S(1)}, f32[1,1024]{1,0:T(1,128)}, u32[]{:S(2)}) copy-start(f32[1,1024]{1,0:T(1,128)} %get-tuple-element.19) | copy-start | bytes 12292

commit v2 on v1

v2 whole, which is shorter than its diff:
```python
import functools

import jax
import jax.numpy as jnp
from jax import lax
from jax.experimental import pallas as pl
from jax.experimental.pallas import tpu as pltpu
from jax.sharding import PartitionSpec as P

MESH = pl.DeviceIdType.MESH
BF = jnp.bfloat16
F32 = jnp.float32


def dot(a, b, dims=((1,), (0,)), **kw):
    return lax.dot_general(a, b, (dims, ((), ())), preferred_element_type=F32, **kw)


def xor_row(row, dz):
    out, bit = 0, 1
    while bit < 8:
        out = out + bit * (((row // bit) % 2 + (dz // bit) % 2) % 2)
        bit *= 2
    return out


def kernel(
    n_row, n_col, cap, fb,
    tok_ref, og_ref, ids_ref, logit_ref, rw_ref, wi_hbm, wo_hbm,
    dtok_ref, drouter_ref, routed_hbm, scaled_hbm, hid_hbm, hgr_hbm,
    wi, wo, send_t, send_s, recv_t, recv_s, gout, gback, hid, hgr, acc,
    rwrecv, rwmat, scsend, screcv, scmat, drsend, drrecv, drsum, drz,
    wsem, osem, ssem, rt_sem, rs_sem, rg_sem, small_sem,
):
    n = n_row * n_col
    row = lax.axis_index("row")
    col = lax.axis_index("col")
    me = row * n_col + col
    tok, width = tok_ref.shape
    ffn = wi.shape[1]
    crows = n_col * cap

    def rows_of(dev):
        return pl.ds(pl.multiple_of(dev * cap, cap), cap)

    def chunk_of(r):
        return pl.ds(pl.multiple_of(r * crows, crows), crows)

    def rows_at(c):
        return pl.ds(c * n_row, n_row)

    load_i = pltpu.make_async_copy(wi_hbm.at[0], wi, wsem.at[0])
    load_o = pltpu.make_async_copy(wo_hbm.at[0], wo, wsem.at[1])
    load_i.start()
    load_o.start()

    barrier = pltpu.get_barrier_semaphore()

    def greet(k, c):
        peer = lax.rem(me + k, n)
        pl.semaphore_signal(
            barrier, inc=1, device_id=(peer // n_col, lax.rem(peer, n_col)),
            device_id_type=MESH)
        return c
    lax.fori_loop(1, n, greet, 0)

    ids = ids_ref[...]
    chosen = (ids == lax.broadcasted_iota(jnp.int32, (n, tok), 0)).astype(F32)
    logits = logit_ref[...]
    ex = jnp.exp(logits - jnp.max(logits, axis=0, keepdims=True))
    probs = ex / jnp.sum(ex, axis=0, keepdims=True)
    gate = jnp.sum(probs * chosen, axis=0, keepdims=True)
    it0 = lax.broadcasted_iota(jnp.int32, (tok, tok), 0)
    it1 = lax.broadcasted_iota(jnp.int32, (tok, tok), 1)
    earlier = dot(chosen.astype(BF), (it0 < it1).astype(F32).astype(BF))
    rank = jnp.sum(earlier * chosen, axis=0, keepdims=True)
    slot = ids.astype(F32) * cap + rank

    def upright(x):
        return jnp.sum(jnp.where(it0 == it1, x, 0.0), axis=1, keepdims=True)

    tokens = tok_ref[...]
    scaled = (upright(gate) * og_ref[...].astype(F32)).astype(BF)

    def fill(r):
        at = lax.broadcasted_iota(jnp.int32, (crows, tok), 0).astype(F32) + (
            r * crows).astype(F32)
        pick = (at == slot).astype(F32).astype(BF)
        send_t[chunk_of(r), :] = dot(pick, tokens).astype(BF)
        send_s[chunk_of(r), :] = dot(pick, scaled).astype(BF)

    def push(src, dst, sem, rsem, dev):
        pltpu.make_async_remote_copy(
            src_ref=src, dst_ref=dst, send_sem=sem, recv_sem=rsem,
            device_id=dev, device_id_type=MESH,
        ).start()

    def col_loop(first, last, body):
        def step(j, c):
            body(lax.rem(col + j, n_col))
            return c
        lax.fori_loop(first, last, step, 0)

    def dispatch(dz):
        r = xor_row(row, dz)

        def send(c):
            peer = rows_of(r * n_col + c)
            push(send_t.at[peer], recv_t.at[rows_of(me)], ssem.at[0], rt_sem.at[dz], (r, c))
            push(send_s.at[peer], recv_s.at[rows_of(me)], ssem.at[1], rs_sem.at[dz], (r, c))
        col_loop(0 if dz else 1, n_col, send)

    half = n_row // 2
    near, far = list(range(half)), list(range(half, n_row))
    for dz in far[:1] + near + far[1:]:
        fill(xor_row(row, dz))
        if dz == far[0]:
            pl.semaphore_wait(barrier, n - 1)
        if dz == 0:
            pltpu.make_async_copy(
                send_t.at[rows_of(me)], recv_t.at[rows_of(me)], rt_sem.at[0]).start()
            pltpu.make_async_copy(
                send_s.at[rows_of(me)], recv_s.at[rows_of(me)], rs_sem.at[0]).start()
        dispatch(dz)

    mine = col * n_row + row
    rwrecv[pl.ds(mine, 1)] = rw_ref[...].astype(F32)[None]
    for k in range(1, n_row):
        push(rwrecv.at[mine], rwrecv.at[mine], ssem.at[3], small_sem.at[0],
             (lax.rem(row + k, n_row), col))

    def wait_rows(ref, sl, sem):
        pltpu.make_async_copy(ref.at[sl], ref.at[sl], sem).wait()

    load_i.wait()
    load_o.wait()
    eye = (lax.broadcasted_iota(jnp.int32, (crows, crows), 0)
           == lax.broadcasted_iota(jnp.int32, (crows, crows), 1))

    def give(dz, first, last):
        r = xor_row(row, dz)

        def send(c):
            push(gout.at[rows_of(r * n_col + c)], gback.at[rows_of(me)],
                 ssem.at[2], rg_sem.at[dz], (r, c))
        col_loop(first, last, send)

    held = []
    for dz in near + far:
        r = xor_row(row, dz)
        sl = chunk_of(r)
        wait_rows(recv_t, sl, rt_sem.at[dz])
        wait_rows(recv_s, sl, rs_sem.at[dz])
        if dz == far[-1]:
            for before in held:
                give(before, n_col // 2, n_col)
        acc[...] = jnp.zeros_like(acc)

        def block(f, v, sl=sl):
            fs = pl.ds(pl.multiple_of(f * fb, fb), fb)
            w1 = wi[:, fs]
            pre = dot(recv_t[sl, :], w1)
            back = dot(recv_s[sl, :], wo[fs, :], ((1,), (1,)))
            h = jnp.maximum(pre, 0.0).astype(BF)
            g = jnp.where(pre > 0.0, back, 0.0).astype(BF)
            hid[sl, fs] = h
            hgr[sl, fs] = g
            acc[...] += dot(g, w1, ((1,), (1,)))
            return v + jnp.sum(h.astype(F32) * back, axis=1, keepdims=True)

        v = lax.fori_loop(0, ffn // fb, block, jnp.zeros((crows, 1), F32))
        gout[sl, :] = acc[...].astype(BF)
        scsend[pl.ds(r, 1)] = jnp.sum(
            jnp.where(eye, v, 0.0), axis=0, keepdims=True)[None]

        def tell(c, r=r):
            push(scsend.at[r], screcv.at[me], ssem.at[4], small_sem.at[1], (r, c))
        if dz == 0:
            pltpu.make_async_copy(
                gout.at[rows_of(me)], gback.at[rows_of(me)], rg_sem.at[0]).start()
            pltpu.make_async_copy(scsend.at[r], screcv.at[me], small_sem.at[1]).start()
        col_loop(0 if dz else 1, n_col, tell)
        if dz in far[:-1]:
            give(dz, 0, n_col // 2)
            held.append(dz)
        else:
            give(dz, 0 if dz else 1, n_col)
        if dz == 0:
            wait_rows(rwrecv, pl.ds(0, n_row - 1), small_sem.at[0])

            def pass_on(c):
                push(rwrecv.at[rows_at(col)], rwrecv.at[rows_at(col)],
                     ssem.at[6], small_sem.at[3], (row, c))
            col_loop(1, n_col, pass_on)
        for k, (src, dst) in enumerate((
                (recv_t, routed_hbm), (recv_s, scaled_hbm), (hid, hid_hbm), (hgr, hgr_hbm))):
            pltpu.make_async_copy(src.at[sl], dst.at[sl], osem.at[k]).start()

    pltpu.make_async_copy(screcv, screcv, small_sem.at[1]).wait()
    for e in range(n):
        scmat[e:e + 1, :] = screcv[e]
    picked = dot(scmat[...], chosen, ((0,), (0,)), precision=lax.Precision.HIGHEST)
    lane = lax.broadcasted_iota(jnp.int32, (crows, tok), 0).astype(F32)
    own = (col * cap).astype(F32) + rank
    vg = jnp.sum(jnp.where(lane == own, picked, 0.0), axis=0, keepdims=True)
    lg = (vg * (chosen - probs)).astype(BF)
    part = dot(lg, tokens)
    for e in range(n):
        drsend[(e % n_col) * n_row + e // n_col] = part[e:e + 1, :]

    def gather_part(c):
        push(drsend.at[rows_at(c)], drrecv.at[rows_at(col)],
             ssem.at[5], small_sem.at[2], (row, c))
    col_loop(1, n_col, gather_part)
    drrecv[rows_at(col)] = drsend[rows_at(col)]

    others = pl.ds(0, n - n_row)
    wait_rows(rwrecv, others, small_sem.at[3])
    for e in range(n):
        rwmat[e:e + 1, :] = rwrecv[(e % n_col) * n_row + e // n_col]
    router_part = dot(lg, rwmat[...].astype(BF), ((0,), (0,)))

    wait_rows(drrecv, others, small_sem.at[2])
    total = drrecv[0:n_row]
    for c in range(1, n_col):
        total = total + drrecv[c * n_row:(c + 1) * n_row]
    drsum[...] = total
    for k in range(1, n_row):
        r = lax.rem(row + k, n_row)
        push(drsum.at[r], drz.at[row], ssem.at[7], small_sem.at[4], (r, col))
    drz[pl.ds(row, 1)] = drsum[pl.ds(row, 1)]

    at = lax.broadcasted_iota(jnp.int32, (tok, n * cap), 1).astype(F32)
    pick = (at == upright(slot)).astype(F32).astype(BF)
    for dz in near + far:
        wait_rows(gback, chunk_of(xor_row(row, dz)), rg_sem.at[dz])
    dtok_ref[...] = (dot(pick, gback[...]) + router_part).astype(BF)

    wait_rows(drz, pl.ds(0, n_row - 1), small_sem.at[4])
    drouter_ref[...] = jnp.sum(drz[...], axis=0)

    most = pl.ds(0, (n - 1) * cap)
    wait_rows(send_t, most, ssem.at[0])
    wait_rows(send_s, most, ssem.at[1])
    wait_rows(gout, most, ssem.at[2])
    wait_rows(rwrecv, pl.ds(0, n_row - 1), ssem.at[3])
    wait_rows(screcv, pl.ds(0, n - 1), ssem.at[4])
    wait_rows(drsend, others, ssem.at[5])
    wait_rows(rwrecv, others, ssem.at[6])
    wait_rows(drsum, pl.ds(0, n_row - 1), ssem.at[7])
    for k, (src, dst) in enumerate((
            (recv_t, routed_hbm), (recv_s, scaled_hbm), (hid, hid_hbm), (hgr, hgr_hbm))):
        pltpu.make_async_copy(src, dst, osem.at[k]).wait()


def weight_grads(routed, scaled, hid, hgr, dtok, drouter, dwi, dwo, dtok_out, drouter_out):
    dwi[0] = dot(routed[...], hgr[...], ((0,), (0,))).astype(BF)
    dwo[0] = dot(hid[...], scaled[...], ((0,), (0,))).astype(BF)
    dtok_out[...] = dtok[...]
    drouter_out[...] = drouter[...]


def per_device(tokens, out_grad, expert_ids, router_logits, router_weight, w_in, w_out):
    n_row = lax.axis_size("row")
    n_col = lax.axis_size("col")
    n = n_row * n_col
    tok, width = tokens.shape
    ffn = w_in.shape[2]
    cap = max(16, 2 * tok // n)
    rows = n * cap
    crows = n_col * cap
    vm = pl.BlockSpec(memory_space=pltpu.VMEM)
    hbm = pl.BlockSpec(memory_space=pl.ANY)
    dma = pltpu.SemaphoreType.DMA
    big = pltpu.VMEM((rows, width), BF)
    line = pltpu.VMEM((n, 1, width), F32)
    few = pltpu.VMEM((n_row, 1, width), F32)
    limit = 60 * 1024 * 1024
    shape = jax.ShapeDtypeStruct
    d_tokens, d_router, routed, scaled, hid, hgr = pl.pallas_call(
        functools.partial(kernel, n_row, n_col, cap, min(512, ffn)),
        out_shape=(
            shape((tok, width), BF),
            shape((1, width), F32),
            shape((rows, width), BF),
            shape((rows, width), BF),
            shape((rows, ffn), BF),
            shape((rows, ffn), BF),
        ),
        in_specs=[vm] * 5 + [hbm] * 2,
        out_specs=(vm, vm, hbm, hbm, hbm, hbm),
        scratch_shapes=[
            pltpu.VMEM((width, ffn), BF),
            pltpu.VMEM((ffn, width), BF),
            big, big, big, big, big, big,
            pltpu.VMEM((rows, ffn), BF),
            pltpu.VMEM((rows, ffn), BF),
            pltpu.VMEM((crows, width), F32),
            line,
            pltpu.VMEM((n, width), F32),
            pltpu.VMEM((n_row, 1, crows), F32),
            pltpu.VMEM((n, 1, crows), F32),
            pltpu.VMEM((n, crows), F32),
            line, line, few, few,
            dma((2,)),
            dma((4,)),
            dma((8,)),
            dma((n_row,)),
            dma((n_row,)),
            dma((n_row,)),
            dma((5,)),
        ],
        compiler_params=pltpu.CompilerParams(
            collective_id=0, has_side_effects=True, vmem_limit_bytes=limit
        ),
        cost_estimate=pl.CostEstimate(
            flops=6 * rows * width * ffn, bytes_accessed=8 * width * ffn, transcendentals=0
        ),
    )(tokens, out_grad, expert_ids[None, :], router_logits.T, router_weight, w_in, w_out)

    steps = 4
    d_wi, d_wo, d_tokens, d_router = pl.pallas_call(
        weight_grads,
        grid=(steps,),
        out_shape=(
            shape(w_in.shape, BF),
            shape(w_out.shape, BF),
            shape((tok, width), BF),
            shape((1, width), F32),
        ),
        in_specs=[
            pl.BlockSpec((rows, width // steps), lambda i: (0, i)),
            pl.BlockSpec((rows, width), lambda i: (0, 0)),
            pl.BlockSpec((rows, ffn // steps), lambda i: (0, i)),
            pl.BlockSpec((rows, ffn), lambda i: (0, 0)),
            pl.BlockSpec((tok // steps, width), lambda i: (i, 0)),
            pl.BlockSpec((1, width), lambda i: (0, 0)),
        ],
        out_specs=(
            pl.BlockSpec((1, width // steps, ffn), lambda i: (0, i, 0)),
            pl.BlockSpec((1, ffn // steps, width), lambda i: (0, i, 0)),
            pl.BlockSpec((tok // steps, width), lambda i: (i, 0)),
            pl.BlockSpec((1, width), lambda i: (0, 0)),
        ),
        compiler_params=pltpu.CompilerParams(vmem_limit_bytes=limit),
        cost_estimate=pl.CostEstimate(
            flops=4 * rows * width * ffn, bytes_accessed=6 * width * ffn, transcendentals=0
        ),
    )(routed, scaled, hid, hgr, d_tokens, d_router)
    return d_tokens, d_wi, d_wo, d_router


def solution(mesh):
    both = ("row", "col")
    flat, cube = P(both, None), P(both, None, None)
    return jax.shard_map(
        per_device,
        mesh=mesh,
        in_specs=(flat, flat, P(both), flat, flat, cube, cube),
        out_specs=(flat, cube, cube, flat),
        check_vma=False,
    )
```

time: 102 us -> 102 us (level)
  Pallas kernels: 88.5 us -> 102 us
  local copies, waits for them, and re-layouts: 12.4 us -> 0 us
    unnamed x9 -> x0, local copies, waits for them, and re-layouts: 10.9 us -> none
    pallas_call x0 -> x1, Pallas kernels: none -> 8.88 us  [per_device(): pl.pallas_call(weight_grads, grid=(steps,), out_shape=(shape(w_in.shape,...]
    pallas_call x1, Pallas kernels: 88.5 us -> 92.7 us  [per_device(): pl.pallas_call(functools.partial(kernel, n_row, n_col, cap, min(512, ffn)...]
    broadcast_in_dim x1 -> x0, local copies, waits for them, and re-layouts: 1.47 us -> none  [per_device(): expert_ids[:, None]]
where the time goes in v2:
time: 102 us
  Pallas kernels  102 us (100%)
    pallas_call x1, Pallas kernels, per_device(): pl.pallas_call(functools.partial(kernel, n_row, n_col, cap, min(512, ffn)...  92.7 us
    pallas_call x1, Pallas kernels, per_device(): pl.pallas_call(weight_grads, grid=(steps,), out_shape=(shape(w_in.shape,...  8.88 us

profile of v2, /device:TPU:0, one launch (start us, length us, event | category | flops | bytes accessed | tf_op | source)
XLA Modules:
  0.0 102.2 jit_solution(12910035993392284600)
XLA Ops:
  0.6 92.7 %shard_map.102 = (bf16[256,1024]{1,0:T(8,128)(2,1)}, f32[1,1024]{1,0:T(1,128)}, bf16[512,1024]{1,0:T(8,128)(2,1)}, bf16[512,1024]{1,0:T(8,128)(2,1)}, bf16[512,2...) custom-call(bf16[256,1024]{1,0:T(8,128)(2,1)} %tok_ref.1, bf16[256,1024]{1,0:T(8,128)(2,1)} %og_ref.1, s32[1,256]{1,0:T(1,128)} %bitcast.3, ...), custom_call_target="tpu_custom_call" | custom-call | flops 6442450944 | bytes 16777216 | tf_op jit(solution)/shard_map/pallas_call | solution.py:280
  93.3 8.9 %shard_map.103 = (bf16[1,1024,2048]{2,1,0:T(8,128)(2,1)}, bf16[1,2048,1024]{2,1,0:T(8,128)(2,1)}, bf16[256,1024]{1,0:T(8,128)(2,1)}, f32[1,1024]{1,0:T(1,128)}) custom-call(bf16[512,1024]{1,0:T(8,128)(2,1)} %get-tuple-element.14.routed, bf16[512,1024]{1,0:T(8,128)(2,1)} %get-tuple-element.15.scaled, bf16[512,2048]{1,0:T(8,128)(2,1)} %get-tuple-element.16.hid, ...), custom_call_target="tpu_custom_call" | custom-call | flops 4294967296 | bytes 12582912 | tf_op jit(solution)/shard_map/pallas_call | solution.py:322

commit v3 on v2

--- a/solution.py
+++ b/solution.py
@@ -27,7 +27,7 @@
 def kernel(
     n_row, n_col, cap, fb,
     tok_ref, og_ref, ids_ref, logit_ref, rw_ref, wi_hbm, wo_hbm,
-    dtok_ref, drouter_ref, routed_hbm, scaled_hbm, hid_hbm, hgr_hbm,
+    dtok_ref, drouter_ref, dwi_hbm, dwo_hbm,
     wi, wo, send_t, send_s, recv_t, recv_s, gout, gback, hid, hgr, acc,
     rwrecv, rwmat, scsend, screcv, scmat, drsend, drrecv, drsum, drz,
     wsem, osem, ssem, rt_sem, rs_sem, rg_sem, small_sem,
@@ -66,28 +66,22 @@
 
     ids = ids_ref[...]
     chosen = (ids == lax.broadcasted_iota(jnp.int32, (n, tok), 0)).astype(F32)
-    logits = logit_ref[...]
-    ex = jnp.exp(logits - jnp.max(logits, axis=0, keepdims=True))
-    probs = ex / jnp.sum(ex, axis=0, keepdims=True)
-    gate = jnp.sum(probs * chosen, axis=0, keepdims=True)
     it0 = lax.broadcasted_iota(jnp.int32, (tok, tok), 0)
     it1 = lax.broadcasted_iota(jnp.int32, (tok, tok), 1)
     earlier = dot(chosen.astype(BF), (it0 < it1).astype(F32).astype(BF))
     rank = jnp.sum(earlier * chosen, axis=0, keepdims=True)
     slot = ids.astype(F32) * cap + rank
+    tokens = tok_ref[...]
 
     def upright(x):
         return jnp.sum(jnp.where(it0 == it1, x, 0.0), axis=1, keepdims=True)
 
-    tokens = tok_ref[...]
-    scaled = (upright(gate) * og_ref[...].astype(F32)).astype(BF)
-
-    def fill(r):
+    def fill(ref, values, dz):
+        r = xor_row(row, dz)
         at = lax.broadcasted_iota(jnp.int32, (crows, tok), 0).astype(F32) + (
             r * crows).astype(F32)
         pick = (at == slot).astype(F32).astype(BF)
-        send_t[chunk_of(r), :] = dot(pick, tokens).astype(BF)
-        send_s[chunk_of(r), :] = dot(pick, scaled).astype(BF)
+        ref[chunk_of(r), :] = dot(pick, values).astype(BF)
 
     def push(src, dst, sem, rsem, dev):
         pltpu.make_async_remote_copy(
@@ -101,27 +95,32 @@
             return c
         lax.fori_loop(first, last, step, 0)
 
-    def dispatch(dz):
-        r = xor_row(row, dz)
-
-        def send(c):
-            peer = rows_of(r * n_col + c)
-            push(send_t.at[peer], recv_t.at[rows_of(me)], ssem.at[0], rt_sem.at[dz], (r, c))
-            push(send_s.at[peer], recv_s.at[rows_of(me)], ssem.at[1], rs_sem.at[dz], (r, c))
-        col_loop(0 if dz else 1, n_col, send)
+    def send_tokens(dz, c):
+        r = xor_row(row, dz)
+        push(send_t.at[rows_of(r * n_col + c)], recv_t.at[rows_of(me)],
+             ssem.at[0], rt_sem.at[dz], (r, c))
+
+    def send_scaled(dz, c):
+        r = xor_row(row, dz)
+        push(send_s.at[rows_of(r * n_col + c)], recv_s.at[rows_of(me)],
+             ssem.at[1], rs_sem.at[dz], (r, c))
+
+    def dispatch(far, near, sends):
+        for send in sends:
+            send(far, col)
+            if near:
+                send(near, col)
+
+        def both(c):
+            for send in sends:
+                send(far, c)
+                send(near, c)
+        col_loop(1, n_col, both)
 
     half = n_row // 2
-    near, far = list(range(half)), list(range(half, n_row))
-    for dz in far[:1] + near + far[1:]:
-        fill(xor_row(row, dz))
-        if dz == far[0]:
-            pl.semaphore_wait(barrier, n - 1)
-        if dz == 0:
-            pltpu.make_async_copy(
-                send_t.at[rows_of(me)], recv_t.at[rows_of(me)], rt_sem.at[0]).start()
-            pltpu.make_async_copy(
-                send_s.at[rows_of(me)], recv_s.at[rows_of(me)], rs_sem.at[0]).start()
-        dispatch(dz)
+    fill(send_t, tokens, half)
+    fill(send_t, tokens, 0)
+    pl.semaphore_wait(barrier, n - 1)
 
     mine = col * n_row + row
     rwrecv[pl.ds(mine, 1)] = rw_ref[...].astype(F32)[None]
@@ -129,6 +128,26 @@
         push(rwrecv.at[mine], rwrecv.at[mine], ssem.at[3], small_sem.at[0],
              (lax.rem(row + k, n_row), col))
 
+    dispatch(half, 0, (send_tokens,))
+    pltpu.make_async_copy(
+        send_t.at[rows_of(me)], recv_t.at[rows_of(me)], rt_sem.at[0]).start()
+
+    logits = logit_ref[...]
+    ex = jnp.exp(logits - jnp.max(logits, axis=0, keepdims=True))
+    probs = ex / jnp.sum(ex, axis=0, keepdims=True)
+    gate = jnp.sum(probs * chosen, axis=0, keepdims=True)
+    scaled = (upright(gate) * og_ref[...].astype(F32)).astype(BF)
+    fill(send_s, scaled, half)
+    fill(send_s, scaled, 0)
+    dispatch(half, 0, (send_scaled,))
+    pltpu.make_async_copy(
+        send_s.at[rows_of(me)], recv_s.at[rows_of(me)], rs_sem.at[0]).start()
+    for near in range(1, half):
+        for dz in (half + near, near):
+            fill(send_t, tokens, dz)
+            fill(send_s, scaled, dz)
+        dispatch(half + near, near, (send_tokens, send_scaled))
+
     def wait_rows(ref, sl, sem):
         pltpu.make_async_copy(ref.at[sl], ref.at[sl], sem).wait()
 
@@ -145,15 +164,12 @@
                  ssem.at[2], rg_sem.at[dz], (r, c))
         col_loop(first, last, send)
 
-    held = []
-    for dz in near + far:
+    turns = [dz for near in range(half) for dz in (near, half + near)]
+    for dz in turns:
         r = xor_row(row, dz)
         sl = chunk_of(r)
         wait_rows(recv_t, sl, rt_sem.at[dz])
         wait_rows(recv_s, sl, rs_sem.at[dz])
-        if dz == far[-1]:
-            for before in held:
-                give(before, n_col // 2, n_col)
         acc[...] = jnp.zeros_like(acc)
 
         def block(f, v, sl=sl):
@@ -180,21 +196,14 @@
                 gout.at[rows_of(me)], gback.at[rows_of(me)], rg_sem.at[0]).start()
             pltpu.make_async_copy(scsend.at[r], screcv.at[me], small_sem.at[1]).start()
         col_loop(0 if dz else 1, n_col, tell)
-        if dz in far[:-1]:
-            give(dz, 0, n_col // 2)
-            held.append(dz)
-        else:
-            give(dz, 0 if dz else 1, n_col)
-        if dz == 0:
+        give(dz, 0 if dz else 1, n_col)
+        if dz == half:
             wait_rows(rwrecv, pl.ds(0, n_row - 1), small_sem.at[0])
 
             def pass_on(c):
                 push(rwrecv.at[rows_at(col)], rwrecv.at[rows_at(col)],
                      ssem.at[6], small_sem.at[3], (row, c))
             col_loop(1, n_col, pass_on)
-        for k, (src, dst) in enumerate((
-                (recv_t, routed_hbm), (recv_s, scaled_hbm), (hid, hid_hbm), (hgr, hgr_hbm))):
-            pltpu.make_async_copy(src.at[sl], dst.at[sl], osem.at[k]).start()
 
     pltpu.make_async_copy(screcv, screcv, small_sem.at[1]).wait()
     for e in range(n):
@@ -214,6 +223,15 @@
     col_loop(1, n_col, gather_part)
     drrecv[rows_at(col)] = drsend[rows_at(col)]
 
+    db = min(256, width)
+
+    def grad_in_w(i, c):
+        ds = pl.ds(pl.multiple_of(i * db, db), db)
+        wi[ds, :] = dot(recv_t[:, ds], hgr[...], ((0,), (0,))).astype(BF)
+        pltpu.make_async_copy(wi.at[ds], dwi_hbm.at[0, ds], osem.at[0]).start()
+        return c
+    lax.fori_loop(0, width // db, grad_in_w, 0)
+
     others = pl.ds(0, n - n_row)
     wait_rows(rwrecv, others, small_sem.at[3])
     for e in range(n):
@@ -230,9 +248,16 @@
         push(drsum.at[r], drz.at[row], ssem.at[7], small_sem.at[4], (r, col))
     drz[pl.ds(row, 1)] = drsum[pl.ds(row, 1)]
 
+    def grad_out_w(i, c):
+        fs = pl.ds(pl.multiple_of(i * fb, fb), fb)
+        wo[fs, :] = dot(hid[:, fs], recv_s[...], ((0,), (0,))).astype(BF)
+        pltpu.make_async_copy(wo.at[fs], dwo_hbm.at[0, fs], osem.at[1]).start()
+        return c
+    lax.fori_loop(0, ffn // fb, grad_out_w, 0)
+
     at = lax.broadcasted_iota(jnp.int32, (tok, n * cap), 1).astype(F32)
     pick = (at == upright(slot)).astype(F32).astype(BF)
-    for dz in near + far:
+    for dz in turns:
         wait_rows(gback, chunk_of(xor_row(row, dz)), rg_sem.at[dz])
     dtok_ref[...] = (dot(pick, gback[...]) + router_part).astype(BF)
 
@@ -248,16 +273,15 @@
     wait_rows(drsend, others, ssem.at[5])
     wait_rows(rwrecv, others, ssem.at[6])
     wait_rows(drsum, pl.ds(0, n_row - 1), ssem.at[7])
-    for k, (src, dst) in enumerate((
-            (recv_t, routed_hbm), (recv_s, scaled_hbm), (hid, hid_hbm), (hgr, hgr_hbm))):
-        pltpu.make_async_copy(src, dst, osem.at[k]).wait()
-
-
-def weight_grads(routed, scaled, hid, hgr, dtok, drouter, dwi, dwo, dtok_out, drouter_out):
-    dwi[0] = dot(routed[...], hgr[...], ((0,), (0,))).astype(BF)
-    dwo[0] = dot(hid[...], scaled[...], ((0,), (0,))).astype(BF)
+    pltpu.make_async_copy(wi, dwi_hbm.at[0], osem.at[0]).wait()
+    pltpu.make_async_copy(wo, dwo_hbm.at[0], osem.at[1]).wait()
+
+
+def hand_over(dtok, drouter, dwi, dwo, dtok_out, drouter_out, dwi_out, dwo_out):
     dtok_out[...] = dtok[...]
     drouter_out[...] = drouter[...]
+    dwi_out[...] = dwi[...]
+    dwo_out[...] = dwo[...]
 
 
 def per_device(tokens, out_grad, expert_ids, router_logits, router_weight, w_in, w_out):
@@ -277,18 +301,17 @@
     few = pltpu.VMEM((n_row, 1, width), F32)
     limit = 60 * 1024 * 1024
     shape = jax.ShapeDtypeStruct
-    d_tokens, d_router, routed, scaled, hid, hgr = pl.pallas_call(
+    shapes = (
+        shape((tok, width), BF),
+        shape((1, width), F32),
+        shape(w_in.shape, BF),
+        shape(w_out.shape, BF),
+    )
+    results = pl.pallas_call(
         functools.partial(kernel, n_row, n_col, cap, min(512, ffn)),
-        out_shape=(
-            shape((tok, width), BF),
-            shape((1, width), F32),
-            shape((rows, width), BF),
-            shape((rows, width), BF),
-            shape((rows, ffn), BF),
-            shape((rows, ffn), BF),
-        ),
+        out_shape=shapes,
         in_specs=[vm] * 5 + [hbm] * 2,
-        out_specs=(vm, vm, hbm, hbm, hbm, hbm),
+        out_specs=(vm, vm, hbm, hbm),
         scratch_shapes=[
             pltpu.VMEM((width, ffn), BF),
             pltpu.VMEM((ffn, width), BF),
@@ -303,7 +326,7 @@
             pltpu.VMEM((n, crows), F32),
             line, line, few, few,
             dma((2,)),
-            dma((4,)),
+            dma((2,)),
             dma((8,)),
             dma((n_row,)),
             dma((n_row,)),
@@ -314,39 +337,28 @@
             collective_id=0, has_side_effects=True, vmem_limit_bytes=limit
         ),
         cost_estimate=pl.CostEstimate(
-            flops=6 * rows * width * ffn, bytes_accessed=8 * width * ffn, transcendentals=0
+            flops=10 * rows * width * ffn, bytes_accessed=8 * width * ffn, transcendentals=0
         ),
     )(tokens, out_grad, expert_ids[None, :], router_logits.T, router_weight, w_in, w_out)
 
-    steps = 4
-    d_wi, d_wo, d_tokens, d_router = pl.pallas_call(
-        weight_grads,
+    steps = 8
+    blocks = (
+        pl.BlockSpec((tok // steps, width), lambda i: (i, 0)),
+        pl.BlockSpec((1, width), lambda i: (0, 0)),
+        pl.BlockSpec((1, width // steps, ffn), lambda i: (0, i, 0)),
+        pl.BlockSpec((1, ffn // steps, width), lambda i: (0, i, 0)),
+    )
+    d_tokens, d_router, d_wi, d_wo = pl.pallas_call(
+        hand_over,
         grid=(steps,),
-        out_shape=(
-            shape(w_in.shape, BF),
-            shape(w_out.shape, BF),
-            shape((tok, width), BF),
-            shape((1, width), F32),
-        ),
-        in_specs=[
-            pl.BlockSpec((rows, width // steps), lambda i: (0, i)),
-            pl.BlockSpec((rows, width), lambda i: (0, 0)),
-            pl.BlockSpec((rows, ffn // steps), lambda i: (0, i)),
-            pl.BlockSpec((rows, ffn), lambda i: (0, 0)),
-            pl.BlockSpec((tok // steps, width), lambda i: (i, 0)),
-            pl.BlockSpec((1, width), lambda i: (0, 0)),
-        ],
-        out_specs=(
-            pl.BlockSpec((1, width // steps, ffn), lambda i: (0, i, 0)),
-            pl.BlockSpec((1, ffn // steps, width), lambda i: (0, i, 0)),
-            pl.BlockSpec((tok // steps, width), lambda i: (i, 0)),
-            pl.BlockSpec((1, width), lambda i: (0, 0)),
-        ),
+        out_shape=shapes,
+        in_specs=blocks,
+        out_specs=blocks,
         compiler_params=pltpu.CompilerParams(vmem_limit_bytes=limit),
         cost_estimate=pl.CostEstimate(
-            flops=4 * rows * width * ffn, bytes_accessed=6 * width * ffn, transcendentals=0
+            flops=0, bytes_accessed=8 * width * ffn, transcendentals=0
         ),
-    )(routed, scaled, hid, hgr, d_tokens, d_router)
+    )(*results)
     return d_tokens, d_wi, d_wo, d_router
 
 

time: 102 us -> 92.6 us (0.908)
  Pallas kernels: 102 us -> 91.6 us
    pallas_call x1, Pallas kernels: 92.7 us -> 82.4 us  [per_device(): pl.pallas_call(functools.partial(kernel, n_row, n_col, cap, min(512, ffn)...]
where the time goes in v3:
time: 92.6 us; the launch traced here: 92.2 us
  Pallas kernels  91.6 us (99%)
    pallas_call x1, Pallas kernels, per_device(): pl.pallas_call(functools.partial(kernel, n_row, n_col, cap, min(512, ffn)...  82.4 us
    pallas_call x1, Pallas kernels, per_device(): pl.pallas_call(hand_over, grid=(steps,), out_shape=shapes, in_specs=block...  9.16 us

profile of v3, /device:TPU:0, one launch (start us, length us, event | category | flops | bytes accessed | tf_op | source)
XLA Modules:
  0.0 92.2 jit_solution(16398065694657331704)
XLA Ops:
  0.6 82.4 %shard_map.102 = (bf16[256,1024]{1,0:T(8,128)(2,1)}, f32[1,1024]{1,0:T(1,128)}, bf16[1,1024,2048]{2,1,0:T(8,128)(2,1)}, bf16[1,2048,1024]{2,1,0:T(8,128)(2,1)}) custom-call(bf16[256,1024]{1,0:T(8,128)(2,1)} %tok_ref.1, bf16[256,1024]{1,0:T(8,128)(2,1)} %og_ref.1, s32[1,256]{1,0:T(1,128)} %bitcast.3, f32[32,256]{1,0:T(8,128)} %bitcast.2, ...), custom_call_target="tpu_custom_call" | custom-call | flops 10737418240 | bytes 16777216 | tf_op jit(solution)/shard_map/pallas_call | solution.py:310
  83.1 9.2 %shard_map.103 = (bf16[256,1024]{1,0:T(8,128)(2,1)}, f32[1,1024]{1,0:T(1,128)}, bf16[1,1024,2048]{2,1,0:T(8,128)(2,1)}, bf16[1,2048,1024]{2,1,0:T(8,128)(2,1)}) custom-call(bf16[256,1024]{1,0:T(8,128)(2,1)} %get-tuple-element.12.dtok, f32[1,1024]{1,0:T(1,128)} %get-tuple-element.13.drouter, bf16[1,1024,2048]{2,1,0:T(8,128)(2,1)} %get-tuple-element.14.dwi, ...), custom_call_target="tpu_custom_call" | custom-call | bytes 16777216 | tf_op jit(solution)/shard_map/pallas_call | solution.py:351

commit v4 on v3

--- a/solution.py
+++ b/solution.py
@@ -277,11 +277,18 @@
     pltpu.make_async_copy(wo, dwo_hbm.at[0], osem.at[1]).wait()
 
 
-def hand_over(dtok, drouter, dwi, dwo, dtok_out, drouter_out, dwi_out, dwo_out):
-    dtok_out[...] = dtok[...]
-    drouter_out[...] = drouter[...]
-    dwi_out[...] = dwi[...]
-    dwo_out[...] = dwo[...]
+def hand_over(parts, dtok, drouter, dwi, dwo, dtok_out, drouter_out, dwi_out, dwo_out, sem):
+    copies = [(dtok, dtok_out), (drouter, drouter_out)]
+    for src, dst in ((dwi, dwi_out), (dwo, dwo_out)):
+        step = src.shape[1] // parts
+        for i in range(parts):
+            at = pl.ds(i * step, step)
+            copies.append((src.at[0, at], dst.at[0, at]))
+    copies = [pltpu.make_async_copy(*pair, sem.at[i]) for i, pair in enumerate(copies)]
+    for copy in copies:
+        copy.start()
+    for copy in copies:
+        copy.wait()
 
 
 def per_device(tokens, out_grad, expert_ids, router_logits, router_weight, w_in, w_out):
@@ -299,7 +306,8 @@
     big = pltpu.VMEM((rows, width), BF)
     line = pltpu.VMEM((n, 1, width), F32)
     few = pltpu.VMEM((n_row, 1, width), F32)
-    limit = 60 * 1024 * 1024
+    held = 4 * width * ffn + 2 * rows * (6 * width + 2 * ffn) + 4 * crows * width
+    limit = held + 9 * 1024 * 1024
     shape = jax.ShapeDtypeStruct
     shapes = (
         shape((tok, width), BF),
@@ -310,7 +318,7 @@
     results = pl.pallas_call(
         functools.partial(kernel, n_row, n_col, cap, min(512, ffn)),
         out_shape=shapes,
-        in_specs=[vm] * 5 + [hbm] * 2,
+        in_specs=[vm] * 5 + [pl.BlockSpec(memory_space=pltpu.HBM)] * 2,
         out_specs=(vm, vm, hbm, hbm),
         scratch_shapes=[
             pltpu.VMEM((width, ffn), BF),
@@ -339,24 +347,20 @@
         cost_estimate=pl.CostEstimate(
             flops=10 * rows * width * ffn, bytes_accessed=8 * width * ffn, transcendentals=0
         ),
-    )(tokens, out_grad, expert_ids[None, :], router_logits.T, router_weight, w_in, w_out)
-
-    steps = 8
-    blocks = (
-        pl.BlockSpec((tok // steps, width), lambda i: (i, 0)),
-        pl.BlockSpec((1, width), lambda i: (0, 0)),
-        pl.BlockSpec((1, width // steps, ffn), lambda i: (0, i, 0)),
-        pl.BlockSpec((1, ffn // steps, width), lambda i: (0, i, 0)),
-    )
+    )(tokens, out_grad, expert_ids[None, :], router_logits.T, router_weight,
+      pltpu.with_memory_space_constraint(w_in, pltpu.HBM),
+      pltpu.with_memory_space_constraint(w_out, pltpu.HBM))
+
+    parts = 4
     d_tokens, d_router, d_wi, d_wo = pl.pallas_call(
-        hand_over,
-        grid=(steps,),
+        functools.partial(hand_over, parts),
         out_shape=shapes,
-        in_specs=blocks,
-        out_specs=blocks,
-        compiler_params=pltpu.CompilerParams(vmem_limit_bytes=limit),
+        in_specs=[hbm] * 4,
+        out_specs=[hbm] * 4,
+        scratch_shapes=[dma((2 + 2 * parts,))],
+        compiler_params=pltpu.CompilerParams(vmem_limit_bytes=4 * 1024 * 1024),
         cost_estimate=pl.CostEstimate(
-            flops=0, bytes_accessed=8 * width * ffn, transcendentals=0
+            flops=0, bytes_accessed=4 * width * ffn, transcendentals=0
         ),
     )(*results)
     return d_tokens, d_wi, d_wo, d_router

time: 92.6 us -> 89.1 us (0.962)
  Pallas kernels: 91.6 us -> 83.9 us
  local copies, waits for them, and re-layouts: 0 us -> 4.2 us
    pallas_call x1, Pallas kernels: 9.16 us -> 3.56 us  [per_device(): pl.pallas_call(functools.partial(hand_over, parts), out_shape=shapes, in_...]
    unnamed x0 -> x10, local copies, waits for them, and re-layouts: none -> 4.2 us
    pallas_call x1, Pallas kernels: 82.4 us -> 80.3 us  [per_device(): pl.pallas_call(functools.partial(kernel, n_row, n_col, cap, min(512, ffn)...]
where the time goes in v4:
time: 89.1 us; the launch traced here: 88.7 us
  Pallas kernels  83.9 us (94%)
  local copies, waits for them, and re-layouts  4.2 us (5%)
    pallas_call x1, Pallas kernels, per_device(): pl.pallas_call(functools.partial(kernel, n_row, n_col, cap, min(512, ffn)...  80.3 us
    unnamed x10, local copies, waits for them, and re-layouts  4.2 us
    pallas_call x1, Pallas kernels, per_device(): pl.pallas_call(functools.partial(hand_over, parts), out_shape=shapes, in_...  3.56 us

profile of v4, /device:TPU:0, one launch (start us, length us, event | category | flops | bytes accessed | tf_op | source)
XLA Modules:
  0.0 88.7 jit_solution(1176641894721803158)
XLA Ops:
  0.6 0.0 copy-start
  0.6 1.0 %copy-done = bf16[256,1024]{1,0:T(8,128)(2,1)S(1)} copy-done((bf16[256,1024]{1,0:T(8,128)(2,1)S(1)}, bf16[256,1024]{1,0:T(8,128)(2,1)}, u32[]{:S(2)}) %copy-start) | copy-done | bytes 524312
  1.7 0.0 copy-start.1
  1.7 1.0 %copy-done.1 = bf16[256,1024]{1,0:T(8,128)(2,1)S(1)} copy-done((bf16[256,1024]{1,0:T(8,128)(2,1)S(1)}, bf16[256,1024]{1,0:T(8,128)(2,1)}, u32[]{:S(2)}) %copy-start.1) | copy-done | bytes 524312
  2.7 0.0 copy-start.2
  2.7 0.8 copy-done.2
  3.5 0.0 copy-start.3
  3.5 0.7 copy-done.3
  4.2 0.0 copy-start.4
  4.2 0.7 copy-done.4
  4.8 80.3 %shard_map.102 = (bf16[256,1024]{1,0:T(8,128)(2,1)S(1)}, f32[1,1024]{1,0:T(1,128)S(1)}, bf16[1,1024,2048]{2,1,0:T(8,128)(2,1)S(1)}, bf16[1,2048,1024]{2,1,0:T(8,128)(2,1)S(1)}) custom-call(bf16[256,1024]{1,0:T(8,128)(2,1)S(1)} %copy-done, bf16[256,1024]{1,0:T(8,128)(2,1)S(1)} %copy-done.1, s32[1,256]{1,0:T(1,128)S(1)} %bitcast.3, f32[32,256]{1,0:T(8,128)S(1)} %bitcast.2, ...), custom_call_target="tpu_custom_call" | custom-call | flops 10737418240 | bytes 16777216 | tf_op jit(solution)/shard_map/pallas_call | solution.py:318
  85.2 3.6 %shard_map.103 = (bf16[256,1024]{1,0:T(8,128)(2,1)}, f32[1,1024]{1,0:T(1,128)}, bf16[1,1024,2048]{2,1,0:T(8,128)(2,1)}, bf16[1,2048,1024]{2,1,0:T(8,128)(2,1)}) custom-call(bf16[256,1024]{1,0:T(8,128)(2,1)S(1)} %get-tuple-element.12.dtok, f32[1,1024]{1,0:T(1,128)S(1)} %get-tuple-element.13.drouter, bf16[1,1024,2048]{2,1,0:T(8,128)(2,1)S(1)} %get-tuple-element.14.dwi, ...), custom_call_target="tpu_custom_call" | custom-call | bytes 8388608 | tf_op jit(solution)/shard_map/pallas_call | solution.py:355
Async XLA Ops:
  0.6 1.0 %copy-start = (bf16[256,1024]{1,0:T(8,128)(2,1)S(1)}, bf16[256,1024]{1,0:T(8,128)(2,1)}, u32[]{:S(2)}) copy-start(bf16[256,1024]{1,0:T(8,128)(2,1)} %tok_ref.1) | copy-start | bytes 1572868
  1.7 1.0 %copy-start.1 = (bf16[256,1024]{1,0:T(8,128)(2,1)S(1)}, bf16[256,1024]{1,0:T(8,128)(2,1)}, u32[]{:S(2)}) copy-start(bf16[256,1024]{1,0:T(8,128)(2,1)} %og_ref.1) | copy-start | bytes 1572868
  2.7 0.8 copy-start.2
  3.5 0.7 copy-start.3
  4.2 0.7 copy-start.4

commit v5 on v4

--- a/solution.py
+++ b/solution.py
@@ -347,9 +347,8 @@
         cost_estimate=pl.CostEstimate(
             flops=10 * rows * width * ffn, bytes_accessed=8 * width * ffn, transcendentals=0
         ),
-    )(tokens, out_grad, expert_ids[None, :], router_logits.T, router_weight,
-      pltpu.with_memory_space_constraint(w_in, pltpu.HBM),
-      pltpu.with_memory_space_constraint(w_out, pltpu.HBM))
+    )(*(pltpu.with_memory_space_constraint(x, pltpu.HBM) for x in (
+        tokens, out_grad, expert_ids[None, :], router_logits.T, router_weight, w_in, w_out)))
 
     parts = 4
     d_tokens, d_router, d_wi, d_wo = pl.pallas_call(

time: 89.1 us -> 85.9 us (0.964)
  local copies, waits for them, and re-layouts: 4.2 us -> 0 us
  Pallas kernels: 83.9 us -> 85.1 us
    unnamed x10 -> x0, local copies, waits for them, and re-layouts: 4.2 us -> none
    pallas_call x1, Pallas kernels: 80.3 us -> 81.6 us  [per_device(): pl.pallas_call(functools.partial(kernel, n_row, n_col, cap, min(512, ffn)...]
where the time goes in v5:
time: 85.9 us; the launch traced here: 85.8 us
  Pallas kernels  85.1 us (99%)
    pallas_call x1, Pallas kernels, per_device(): pl.pallas_call(functools.partial(kernel, n_row, n_col, cap, min(512, ffn)...  81.6 us
    pallas_call x1, Pallas kernels, per_device(): pl.pallas_call(functools.partial(hand_over, parts), out_shape=shapes, in_...  3.56 us

profile of v5, /device:TPU:0, one launch (start us, length us, event | category | flops | bytes accessed | tf_op | source)
XLA Modules:
  0.0 85.8 jit_solution(4053327174195854318)
XLA Ops:
  0.6 81.6 %shard_map.102 = (bf16[256,1024]{1,0:T(8,128)(2,1)S(1)}, f32[1,1024]{1,0:T(1,128)S(1)}, bf16[1,1024,2048]{2,1,0:T(8,128)(2,1)S(1)}, bf16[1,2048,1024]{2,1,0:T(8,128)(2,1)S(1)}) custom-call(bf16[256,1024]{1,0:T(8,128)(2,1)} %tok_ref.1, bf16[256,1024]{1,0:T(8,128)(2,1)} %og_ref.1, s32[1,256]{1,0:T(1,128)} %bitcast.3, f32[32,256]{1,0:T(8,128)} %bitcast.2, ...), custom_call_target="tpu_custom_call" | custom-call | flops 10737418240 | bytes 16777216 | tf_op jit(solution)/shard_map/pallas_call | solution.py:318
  82.2 3.6 %shard_map.103 = (bf16[256,1024]{1,0:T(8,128)(2,1)}, f32[1,1024]{1,0:T(1,128)}, bf16[1,1024,2048]{2,1,0:T(8,128)(2,1)}, bf16[1,2048,1024]{2,1,0:T(8,128)(2,1)}) custom-call(bf16[256,1024]{1,0:T(8,128)(2,1)S(1)} %get-tuple-element.12.dtok, f32[1,1024]{1,0:T(1,128)S(1)} %get-tuple-element.13.drouter, bf16[1,1024,2048]{2,1,0:T(8,128)(2,1)S(1)} %get-tuple-element.14.dwi, ...), custom_call_target="tpu_custom_call" | custom-call | bytes 8388608 | tf_op jit(solution)/shard_map/pallas_call | solution.py:354
